TPU v7x, 32 devices: a whole 2x2x4 slice. The times are simulated.
32 devices in a mesh: dp: 8 (over y, x, core), tensor: 4 (over z).
Axes of the slice: x: 2, y: 2, z: 4, core: 2. Of those that a mesh axis runs over, the one named last changes fastest.
Arguments:
- tokens: bfloat16 [8192, 1024], P(('dp', 'tensor')), may hold values from -6 to 6
- document_lengths: int32 [512], replicated, may hold values from 1 to 512, 8192 in all
- query_proj_weight: bfloat16 [1024, 1024], P(None, 'tensor'), may hold values from -0.1875 to 0.1875
- query_proj_bias: bfloat16 [1024], P('tensor'), may hold values from -3 to 3
- key_proj_weight: bfloat16 [1024, 1024], P(None, 'tensor'), may hold values from -0.1875 to 0.1875
- value_proj_weight: bfloat16 [1024, 1024], P(None, 'tensor'), may hold values from -0.1875 to 0.1875
- value_proj_bias: bfloat16 [1024], P('tensor'), may hold values from -3 to 3
- query_adapter_down: bfloat16 [1024, 8], replicated, may hold values from -0.1875 to 0.1875
- value_adapter_down: bfloat16 [1024, 8], replicated, may hold values from -0.1875 to 0.1875
- query_adapter_up: bfloat16 [8, 1024], P(None, 'tensor'), may hold values from -1 to 1
- value_adapter_up: bfloat16 [8, 1024], P(None, 'tensor'), may hold values from -1 to 1
- attention_out_weight: bfloat16 [1024, 1024], P('tensor'), may hold values from -0.75 to 0.75
- attention_out_bias: bfloat16 [1024], replicated, may hold values from -3 to 3
- attention_norm_gain: bfloat16 [1024], replicated, may hold values from 0.25 to 1.75
- attention_norm_bias: bfloat16 [1024], replicated, may hold values from -3 to 3
- up_proj_weight: bfloat16 [1024, 4096], P(None, 'tensor'), may hold values from -0.1875 to 0.1875
- up_proj_bias: bfloat16 [4096], P('tensor'), may hold values from -3 to 3
- down_proj_weight: bfloat16 [4096, 1024], P('tensor'), may hold values from -0.125 to 0.125
- down_proj_bias: bfloat16 [1024], replicated, may hold values from -3 to 3
- feedforward_norm_gain: bfloat16 [1024], replicated, may hold values from 0.25 to 1.75
- feedforward_norm_bias: bfloat16 [1024], replicated, may hold values from -3 to 3
- cotangent: bfloat16 [8192, 1024], P(('dp', 'tensor')), may hold values from -6 to 6
Outputs:
- output: bfloat16 [8192, 1024], P(('dp', 'tensor'))
- grad_tokens: bfloat16 [8192, 1024], P(('dp', 'tensor'))
- grad_lora_b_query: float32 [8, 1024], P(None, 'tensor')
- grad_lora_b_value: float32 [8, 1024], P(None, 'tensor')
Inputs may be any that keep to these rules, and one draw needn't show every extreme that they name: `document_lengths`: the documents lie one after another over the 8192 positions of the stream and fill it; at least one document has exactly 512 tokens, none has more.
All inputs are finite; a program needn't handle non-finite values.
Results may differ from a plain program's by a relative error of at most 0.017.
The roundings to bfloat16 on the way count: a program that leaves them out, or rounds other values in their place, can miss the bound.
Values may be sent and summed in bfloat16 or wider, within the bound.
A program may use at most 128 MiB of HBM per device.

v0:
```python
import math

import jax
import jax.numpy as jnp
from jax import lax
from jax.sharding import PartitionSpec as P

HD = 64
MAXLEN = 512
QBLK = 512


norm_eps = 1e-05
masked_score = -1e30
adapter_scale = 2.0


def extended(cells, sides, width):
    for axis, dim in sides:
        count = lax.axis_size(axis)
        ends = count - 1
        head = lax.slice_in_dim(cells, 0, width, axis=dim)
        tail = lax.slice_in_dim(cells, cells.shape[dim] - width, cells.shape[dim], axis=dim)
        cells = jnp.concatenate(
            [
                lax.ppermute(tail, axis, [(i, (i + 1) % count) for i in range(ends)]),
                cells,
                lax.ppermute(head, axis, [((i + 1) % count, i) for i in range(ends)]),
            ],
            axis=dim,
        )
    return cells


def layer_norm(input_rows, norm_gain, norm_shift):
    centre = input_rows - jnp.mean(input_rows, axis=-1, keepdims=True)
    variance = jnp.mean(centre * centre, axis=-1, keepdims=True)
    return centre * lax.rsqrt(variance + norm_eps) * norm_gain.astype(
        jnp.float32
    ) + norm_shift.astype(jnp.float32)


def doc_index(document_lengths, positions):
    ends = jnp.cumsum(document_lengths, dtype=jnp.int32)
    passed = jnp.sum(
        (ends[None, :] <= positions[:, None]).astype(jnp.int32), axis=1, dtype=jnp.int32
    )
    inside = (positions >= 0) & (passed < document_lengths.shape[0])
    return jnp.where(inside, passed, -1)


def gelu_exact(input_rows):
    return jax.nn.gelu(input_rows, approximate=False)


def times_transposed(left, right):
    return lax.dot_general(
        left, right, (((1,), (1,)), ((), ())), preferred_element_type=jnp.float32
    )


def shards(
    tokens,
    document_lengths,
    query_proj_weight,
    query_proj_bias,
    key_proj_weight,
    value_proj_weight,
    value_proj_bias,
    query_adapter_down,
    value_adapter_down,
    query_adapter_up,
    value_adapter_up,
    attention_out_weight,
    attention_out_bias,
    attention_norm_gain,
    attention_norm_bias,
    up_proj_weight,
    up_proj_bias,
    down_proj_weight,
    down_proj_bias,
    feedforward_norm_gain,
    feedforward_norm_bias,
    cotangent,
):
    tok_dev = tokens.shape[0]
    group_rows = tok_dev * lax.axis_size("tensor")
    local_width = query_proj_weight.shape[1]
    heads_here = local_width // HD
    adapter_width = query_adapter_up.shape[0]
    window = QBLK + 2 * MAXLEN
    block_count = group_rows // QBLK
    score_scale = 1.0 / math.sqrt(HD)
    group_first = lax.axis_index("dp") * group_rows
    positions = group_first - MAXLEN + jnp.arange(group_rows + 2 * MAXLEN, dtype=jnp.int32)
    key_ids = doc_index(document_lengths, positions)
    query_ids = key_ids[MAXLEN : MAXLEN + group_rows]
    frozen_down_maps = jnp.concatenate([query_adapter_down, value_adapter_down], axis=1)
    adapter_input = jnp.dot(tokens, frozen_down_maps, preferred_element_type=jnp.float32).astype(
        jnp.bfloat16
    )

    def apply_projection(collected_rows, adapter_row_block):
        query_rows = (
            jnp.dot(collected_rows, query_proj_weight, preferred_element_type=jnp.float32)
            + query_proj_bias
        )
        query_rows = query_rows + adapter_scale * jnp.dot(
            adapter_row_block[:, :adapter_width],
            query_adapter_up,
            preferred_element_type=jnp.float32,
        )
        keys_local = jnp.dot(collected_rows, key_proj_weight, preferred_element_type=jnp.float32)
        value_rows_here = (
            jnp.dot(collected_rows, value_proj_weight, preferred_element_type=jnp.float32)
            + value_proj_bias
        )
        value_rows_here = value_rows_here + adapter_scale * jnp.dot(
            adapter_row_block[:, adapter_width:],
            value_adapter_up,
            preferred_element_type=jnp.float32,
        )
        query_value_pair = jnp.concatenate(
            [keys_local.astype(jnp.bfloat16), value_rows_here.astype(jnp.bfloat16)], axis=1
        )
        return (query_rows.astype(jnp.bfloat16), query_value_pair)

    def split_heads(array):
        return array.reshape(array.shape[0], heads_here, HD)

    def scores_of(begin_row, query_rows, pair_ext):
        q_blk = split_heads(lax.dynamic_slice_in_dim(query_rows, begin_row, QBLK, 0))
        pair_win = lax.dynamic_slice_in_dim(pair_ext, begin_row, window, 0)
        k_win = split_heads(pair_win[:, :local_width])
        v_win = split_heads(pair_win[:, local_width:])
        ids_q = lax.dynamic_slice_in_dim(query_ids, begin_row, QBLK, 0)
        ids_k = lax.dynamic_slice_in_dim(key_ids, begin_row, window, 0)
        raw = (
            jnp.einsum("qhd,khd->hqk", q_blk, k_win, preferred_element_type=jnp.float32)
            * score_scale
        )
        allowed = ids_q[:, None] == ids_k[None, :]
        return (jnp.where(allowed[None], raw, masked_score), q_blk, k_win, v_win)

    collected_rows, adapter_row_block = (
        lax.all_gather(tokens, "tensor", axis=0, tiled=True),
        lax.all_gather(adapter_input, "tensor", axis=0, tiled=True),
    )
    query_rows, query_value_pair = apply_projection(collected_rows, adapter_row_block)
    pair_ext = extended(query_value_pair, (("dp", 0),), MAXLEN)

    def forward_block(block_at):
        scores, q_blk, k_win, v_win = scores_of(block_at * QBLK, query_rows, pair_ext)
        row_max = jnp.max(scores, axis=-1, keepdims=True)
        exp_scores = jnp.exp(scores - row_max)
        row_total = jnp.sum(exp_scores, axis=-1, keepdims=True)
        weights = (exp_scores / row_total).astype(jnp.bfloat16)
        out_blk = jnp.einsum("hqk,khd->qhd", weights, v_win, preferred_element_type=jnp.float32)
        return (
            out_blk.reshape(QBLK, local_width).astype(jnp.bfloat16),
            (row_max + jnp.log(row_total))[..., 0],
        )

    attended, log_total = lax.map(forward_block, jnp.arange(block_count, dtype=jnp.int32))
    attended = attended.reshape(group_rows, local_width)
    attn_sum = lax.psum_scatter(
        jnp.dot(attended, attention_out_weight, preferred_element_type=jnp.float32),
        "tensor",
        scatter_dimension=0,
        tiled=True,
    )
    residual_one = tokens.astype(jnp.float32) + attn_sum + attention_out_bias.astype(jnp.float32)

    def norm_first(input_rows):
        return layer_norm(input_rows, attention_norm_gain, attention_norm_bias)

    def norm_second(input_rows):
        return layer_norm(input_rows, feedforward_norm_gain, feedforward_norm_bias)

    middle, norm_first_back = jax.vjp(norm_first, residual_one)
    middle_low = middle.astype(jnp.bfloat16)

    def up_rows(part_rows):
        return jnp.dot(part_rows, up_proj_weight, preferred_element_type=jnp.float32) + up_proj_bias

    before = up_rows(lax.all_gather(middle_low, "tensor", axis=0, tiled=True))
    hidden = gelu_exact(before).astype(jnp.bfloat16)
    ffn_sum = lax.psum_scatter(
        jnp.dot(hidden, down_proj_weight, preferred_element_type=jnp.float32),
        "tensor",
        scatter_dimension=0,
        tiled=True,
    )
    residual_two = middle + ffn_sum + down_proj_bias.astype(jnp.float32)
    final_output, norm_second_back = jax.vjp(norm_second, residual_two)
    output = final_output.astype(jnp.bfloat16)
    (grad_two,) = norm_second_back(cotangent.astype(jnp.float32))
    grad_ffn = grad_two.astype(jnp.bfloat16)
    before_back = up_rows(lax.all_gather(middle_low, "tensor", axis=0, tiled=True))
    toward = times_transposed(
        lax.all_gather(grad_ffn, "tensor", axis=0, tiled=True), down_proj_weight
    )
    _, gelu_back = jax.vjp(gelu_exact, before_back)
    grad_before = gelu_back(toward)[0].astype(jnp.bfloat16)
    grad_middle = grad_two + lax.psum_scatter(
        times_transposed(grad_before, up_proj_weight), "tensor", scatter_dimension=0, tiled=True
    )
    (first_norm_gradient,) = norm_first_back(grad_middle)
    grad_attn = first_norm_gradient.astype(jnp.bfloat16)
    grad_attended = times_transposed(
        lax.all_gather(grad_attn, "tensor", axis=0, tiled=True), attention_out_weight
    ).astype(jnp.bfloat16)
    collected_rows_grad, adapter_backward = (
        lax.all_gather(tokens, "tensor", axis=0, tiled=True),
        lax.all_gather(adapter_input, "tensor", axis=0, tiled=True),
    )
    query_backward, pair_gradient = apply_projection(collected_rows_grad, adapter_backward)
    pair_ext_back = extended(pair_gradient, (("dp", 0),), MAXLEN)

    def backward_block(grad_pairs, block_at):
        begin_row = block_at * QBLK
        scores, q_blk, k_win, v_win = scores_of(begin_row, query_backward, pair_ext_back)
        probs = jnp.exp(scores - log_total[block_at][..., None])
        grad_out_blk = split_heads(lax.dynamic_slice_in_dim(grad_attended, begin_row, QBLK, 0))
        grad_values_win = jnp.einsum(
            "hqk,qhd->khd",
            probs.astype(jnp.bfloat16),
            grad_out_blk,
            preferred_element_type=jnp.float32,
        )
        grad_probs = jnp.einsum(
            "qhd,khd->hqk", grad_out_blk, v_win, preferred_element_type=jnp.float32
        )
        grad_scores = probs * (grad_probs - jnp.sum(grad_probs * probs, axis=-1, keepdims=True))
        grad_scores = grad_scores.astype(jnp.bfloat16)
        grad_queries_blk = (
            jnp.einsum("hqk,khd->qhd", grad_scores, k_win, preferred_element_type=jnp.float32)
            * score_scale
        )
        grad_keys_win = (
            jnp.einsum("hqk,qhd->khd", grad_scores, q_blk, preferred_element_type=jnp.float32)
            * score_scale
        )
        window_grads = jnp.concatenate(
            [
                grad_keys_win.reshape(window, local_width),
                grad_values_win.reshape(window, local_width),
            ],
            axis=1,
        )
        previous = lax.dynamic_slice_in_dim(grad_pairs, begin_row, window, 0)
        grad_pairs = lax.dynamic_update_slice_in_dim(
            grad_pairs, previous + window_grads, begin_row, 0
        )
        return (grad_pairs, grad_queries_blk.reshape(QBLK, local_width))

    grad_pairs_init = jnp.zeros((group_rows + 2 * MAXLEN, 2 * local_width), jnp.float32)
    grad_pairs_ext, grad_query_blocks = lax.scan(
        backward_block, grad_pairs_init, jnp.arange(block_count, dtype=jnp.int32)
    )
    rim_grads = jnp.concatenate(
        [grad_pairs_ext[:MAXLEN], grad_pairs_ext[group_rows + MAXLEN :]], axis=0
    )
    rim_grads_ext = extended(rim_grads.astype(jnp.bfloat16), (("dp", 0),), MAXLEN).astype(
        rim_grads.dtype
    )
    from_lower = jnp.pad(rim_grads_ext[:MAXLEN], ((0, group_rows - MAXLEN), (0, 0)))
    from_upper = jnp.pad(rim_grads_ext[3 * MAXLEN :], ((group_rows - MAXLEN, 0), (0, 0)))
    grad_pairs_own = grad_pairs_ext[MAXLEN : MAXLEN + group_rows] + from_lower + from_upper
    query_rows_gradient = grad_query_blocks.reshape(group_rows, local_width).astype(jnp.bfloat16)
    grad_keys = grad_pairs_own[:, :local_width].astype(jnp.bfloat16)
    value_rows_gradient = grad_pairs_own[:, local_width:].astype(jnp.bfloat16)
    tokens_term = (
        times_transposed(query_rows_gradient, query_proj_weight)
        + times_transposed(grad_keys, key_proj_weight)
        + times_transposed(value_rows_gradient, value_proj_weight)
    )
    adapter_contribution = adapter_scale * jnp.concatenate(
        [
            times_transposed(query_rows_gradient, query_adapter_up),
            times_transposed(value_rows_gradient, value_adapter_up),
        ],
        axis=1,
    )
    token_portion, adapter_portion = (
        lax.psum_scatter(
            tokens_term.astype(jnp.bfloat16), "tensor", scatter_dimension=0, tiled=True
        ).astype(jnp.float32),
        lax.psum_scatter(
            adapter_contribution.astype(jnp.bfloat16), "tensor", scatter_dimension=0, tiled=True
        ).astype(jnp.float32),
    )
    input_rows_gradient = (
        first_norm_gradient
        + token_portion
        + times_transposed(adapter_portion.astype(jnp.bfloat16), frozen_down_maps)
    )
    contract_over_rows = (((0,), (0,)), ((), ()))
    adapter_query_piece = adapter_scale * lax.dot_general(
        adapter_backward[:, :adapter_width],
        query_rows_gradient,
        contract_over_rows,
        preferred_element_type=jnp.float32,
    )
    adapter_value_piece = adapter_scale * lax.dot_general(
        adapter_backward[:, adapter_width:],
        value_rows_gradient,
        contract_over_rows,
        preferred_element_type=jnp.float32,
    )
    query_bias_gradient, value_bias_gradient = lax.psum(
        (adapter_query_piece, adapter_value_piece), "dp"
    )
    return (
        output,
        input_rows_gradient.astype(jnp.bfloat16),
        query_bias_gradient,
        value_bias_gradient,
    )


def solution(mesh):
    return jax.shard_map(
        shards,
        mesh=mesh,
        in_specs=(
            P(("dp", "tensor"), None),
            P(),
            P(None, "tensor"),
            P("tensor"),
            P(None, "tensor"),
            P(None, "tensor"),
            P("tensor"),
            P(),
            P(),
            P(None, "tensor"),
            P(None, "tensor"),
            P("tensor", None),
            P(),
            P(),
            P(),
            P(None, "tensor"),
            P("tensor"),
            P("tensor", None),
            P(),
            P(),
            P(),
            P(("dp", "tensor"), None),
        ),
        out_specs=(
            P(("dp", "tensor"), None),
            P(("dp", "tensor"), None),
            P(None, "tensor"),
            P(None, "tensor"),
        ),
        check_vma=False,
    )
```

profile of v0, /device:TPU:2, one launch (start us, length us, event | category | flops | bytes accessed | tf_op | source)
XLA Modules:
  0.0 700.3 jit_solution(8034863767278230120)
XLA Ops:
  13.5 1.3 fusion.27
  14.7 13.6 %all_gather.19 = bf16[1024,16]{0,1:T(8,128)(2,1)S(1)} all-gather(bf16[256,16]{0,1:T(8,128)(2,1)S(1)} %fusion.27), channel_id=1, replica_groups=mesh['dp'=8,'tensor'=4] {'tensor'}, dimensions={0}, use_global_device_ids=true | all-gather | bytes 40960 | tf_op jit(solution)/shard_map/all_gather | solution.py:147
  28.4 28.7 %all-gather.5.cloned.1.call-done = bf16[1024,1024]{1,0:T(8,128)(2,1)} async-done(((bf16[256,1024]{1,0:T(8,128)(2,1)}), bf16[1024,1024]{1,0:T(8,128)(2,1)}) %all-gather.5.cloned.1.call-update) | async-done | bytes 2097168 | tf_op jit(solution)/shard_map/all_gather | solution.py:146
  57.1 2.6 convolution_add_fusion.2
  60.9 1.9 collective-permute-start
  62.8 3.6 collective-permute-start.1
  67.6 3.8 collective-permute-done
  71.4 4.6 collective-permute-done.1
  76.0 1.5 pad_maximum_fusion
  77.6 33.0 %while.24 = (s32[]{:T(128)}, bf16[2,512,256]{2,1,0:T(8,128)(2,1)}, f32[2,4,512]{2,1,0:T(4,128)S(1)}, s32[2]{0:T(128)S(1)}, bf16[2048,512]{0,1:T(8,128)(2,1)}, /*...) while((s32[]{:T(128)}, bf16[2,512,256]{2,1,0:T(8,128)(2,1)}, ...), condition=%wide.region_6.7_spmd, body=%wide.region_3.6_spmd.sunk | while | flops 843970560 | bytes 47801084 | solution.py:164
  79.5 1.5 constant_dynamic-slice_fusion.9
  81.0 2.5 fusion.122
  83.5 3.5 fusion.123
  87.1 5.2 fusion.124
  96.0 1.5 constant_dynamic-slice_fusion.9
  97.5 2.5 fusion.122
  100.0 3.5 fusion.123
  103.6 5.2 fusion.124
  110.6 4.1 fusion.55
  115.3 75.6 %reduce-scatter.6.cloned.1.call-done = f32[256,1024]{1,0:T(8,128)} async-done(((f32[1024,1024]{1,0:T(8,128)}), f32[256,1024]{1,0:T(8,128)}) %reduce-scatter.6.cloned.1.call-update) | async-done | bytes 1048592 | tf_op jit(solution)/shard_map/reduce_scatter | solution.py:166
  190.9 1.6 fusion.50
  194.1 46.4 %all-gather.7.cloned.1.call-done = bf16[1024,1024]{1,0:T(8,128)(2,1)} async-done(((bf16[256,1024]{1,0:T(8,128)(2,1)}), bf16[1024,1024]{1,0:T(8,128)(2,1)}) %all-gather.7.cloned.1.call-update) | async-done | bytes 2097168 | tf_op jit(solution)/shard_map/all_gather | solution.py:186
  240.4 12.3 %fusion.9 = (f32[1024,1024]{1,0:T(8,128)S(1)}, f32[1024,1024]{1,0:T(8,128)S(1)}) fusion(f32[1024]{0:T(1024)S(1)} %convert_element_type.146, bf16[1024,1024]{1,0:T(8,128)(2,1)} %all-gather.7.cloned.1.call-done, bf16[1024,1024]{1,0:T(8,128)(2,1)S(1)} %copy-done), kind=kOutput, calls=%fused_computation.30 | convolution fusion | flops 2213543936 | bytes 12587008 | tf_op jit(solution)/shard_map/dot_general | solution.py:184
  252.8 1.9 copy-done.41
  254.8 1.3 copy-done.42
  256.1 4.3 fusion.15
  261.1 75.0 %reduce-scatter.8.cloned.1.call-done = f32[256,1024]{1,0:T(8,128)} async-done(((f32[1024,1024]{1,0:T(8,128)}), f32[256,1024]{1,0:T(8,128)}) %reduce-scatter.8.cloned.1.call-update) | async-done | bytes 1048592 | tf_op jit(solution)/shard_map/reduce_scatter | solution.py:188
  336.1 1.7 fusion.49
  337.8 1.4 multiply_reduce_fusion.2
  339.3 1.3 fusion.48
  342.5 46.6 %all-gather.9.cloned.1.call-done = bf16[1024,1024]{1,0:T(8,128)(2,1)} async-done(((bf16[256,1024]{1,0:T(8,128)(2,1)}), bf16[1024,1024]{1,0:T(8,128)(2,1)}) %all-gather.9.cloned.1.call-update) | async-done | bytes 2097168 | tf_op jit(solution)/shard_map/all_gather | solution.py:201
  389.1 11.4 %fusion.21 = f32[1024,1024]{1,0:T(8,128)} fusion(bf16[1024,1024]{1,0:T(8,128)(2,1)S(1)} %copy-done, f32[1024,1024]{1,0:T(8,128)} %copy-done.41, f32[1024,1024]{1,0:T(8,128)} %copy-done.42, f32[1024]{0:T(1024)S(1)} %convert_element_type.146, bf16[1024,1024]{1,0:T(8,128)(2,1)} %all-gather.9.cloned.1.call-done, bf16[1024,1024]{1,0:T(8,128)(2,1)} %param.43), kind=kOutput, calls=%fused_computation.57 | convolution fusion | flops 4310695936 | bytes 18878464 | tf_op jit(solution)/shard_map/dot_general | solution.py:57
  400.5 75.6 %reduce-scatter.10.cloned.1.call-done = f32[256,1024]{1,0:T(8,128)} async-done(((f32[1024,1024]{1,0:T(8,128)}), f32[256,1024]{1,0:T(8,128)}) %reduce-scatter.10.cloned.1.call-update) | async-done | bytes 1048592 | tf_op jit(solution)/shard_map/reduce_scatter | solution.py:205
  476.1 1.6 multiply_reduce_fusion.1
  477.7 1.7 fusion.47
  480.9 46.3 %all-gather.11.cloned.1.call-done = bf16[1024,1024]{1,0:T(8,128)(2,1)} async-done(((bf16[256,1024]{1,0:T(8,128)(2,1)}), bf16[1024,1024]{1,0:T(8,128)(2,1)}) %all-gather.11.cloned.1.call-update) | async-done | bytes 2097168 | tf_op jit(solution)/shard_map/all_gather | solution.py:211
  527.2 3.2 convolution_convert_fusion
  530.4 2.5 broadcast_in_dim.90
  532.9 72.4 %while.25 = (s32[]{:T(128)}, f32[2048,512]{0,1:T(8,128)}, bf16[2,512,256]{2,1,0:T(8,128)(2,1)}, s32[2]{0:T(128)S(1)}, bf16[1024,256]{0,1:T(8,128)(2,1)S(1)}, /*i...) while((s32[]{:T(128)}, f32[2048,512]{0,1:T(8,128)}, ...), condition=%wide.region_20.21_spmd, body=%wide.region_18.20_spmd.sunk | while | flops 2044590080 | bytes 195625488 | solution.py:258
  534.9 1.5 fusion.135
  538.3 6.3 subtract_exponential_fusion.3
  544.9 11.5 %multiply_reduce_fusion.6 = (f32[4,512]{1,0:T(4,128)S(1)}, f32[4,512,1536]{2,1,0:T(8,128)}) fusion(f32[4,512,1536]{2,1,0:T(8,128)} %subtract_exponential_fusion.3, bf16[512,4,64]{0,2,1:T(8,128)(2,1)S(1)} %bitcast.136, bf16[1536,4,64]{0,2,1:T(8,128)(2,1)S(1)} %bitcast.132), kind=kOutput, calls=%fused_computation.15.clone.1 | convolution fusion | flops 408942592 | bytes 26222592 | tf_op jit(solution)/shard_map/while/body/eval_jaxpr/qhd,khd->hqk/dot_general | solution.py:231
  556.4 5.6 multiply_convert_fusion.4
  563.2 1.3 fusion.136
  566.1 2.0 convolution_multiply_fusion.9
  571.1 1.5 fusion.135
  574.6 6.3 subtract_exponential_fusion.3
  581.1 11.5 %multiply_reduce_fusion.6 = (f32[4,512]{1,0:T(4,128)S(1)}, f32[4,512,1536]{2,1,0:T(8,128)}) fusion(f32[4,512,1536]{2,1,0:T(8,128)} %subtract_exponential_fusion.3, bf16[512,4,64]{0,2,1:T(8,128)(2,1)S(1)} %bitcast.136, bf16[1536,4,64]{0,2,1:T(8,128)(2,1)S(1)} %bitcast.132), kind=kOutput, calls=%fused_computation.15.clone.1 | convolution fusion | flops 408942592 | bytes 26222592 | tf_op jit(solution)/shard_map/while/body/eval_jaxpr/qhd,khd->hqk/dot_general | solution.py:231
  592.6 5.6 multiply_convert_fusion.4
  599.4 1.3 fusion.136
  602.4 2.0 convolution_multiply_fusion.9
  605.4 2.6 convert.10
  608.1 1.9 collective-permute-start.2
  610.0 3.9 collective-permute-start.3
  614.2 2.7 fusion.56
  616.9 1.7 collective-permute-done.2
  618.6 4.6 collective-permute-done.3
  624.9 2.8 fusion.30
  628.6 6.0 add_convert_fusion
  634.7 1.2 convolution_multiply_fusion.5
  635.9 1.3 convolution_multiply_fusion.4
  637.2 22.8 %all-reduce.1 = (f32[8,256]{1,0:T(8,128)}, f32[8,256]{1,0:T(8,128)}) all-reduce(f32[8,256]{1,0:T(8,128)S(1)} %convolution_multiply_fusion.5, f32[8,256]{1,0:T(8,128)S(1)} %convolution_multiply_fusion.4), channel_id=1, replica_groups=mesh['dp'=8,'tensor'=4] {'dp'}, use_global_device_ids=true, to_apply=%region_23.24 | all-reduce | flops 4096 | bytes 32768 | tf_op jit(solution)/shard_map/psum | solution.py:311
  660.0 31.2 %reduce-scatter.12.cloned.1.call-done = bf16[256,1024]{1,0:T(8,128)(2,1)} async-done(((bf16[1024,1024]{1,0:T(8,128)(2,1)}), bf16[256,1024]{1,0:T(8,128)(2,1)}) %reduce-scatter.12.cloned.1.call-update) | async-done | bytes 524304 | tf_op jit(solution)/shard_map/reduce_scatter | solution.py:286
  691.2 2.2 fusion.24
  (215 shorter events, 34.6 us)
Async XLA Ops:
  7.2 233.3 %copy-start = (bf16[1024,1024]{1,0:T(8,128)(2,1)S(1)}, bf16[1024,1024]{1,0:T(8,128)(2,1)}, u32[]{:S(2)}) copy-start(bf16[1024,1024]{1,0:T(8,128)(2,1)} %param.41) | copy-start | bytes 6291460
  7.2 52.5 %copy-start.29 = (bf16[8,256]{1,0:T(8,128)(2,1)S(1)}, bf16[8,256]{1,0:T(8,128)(2,1)}, u32[]{:S(2)}) copy-start(bf16[8,256]{1,0:T(8,128)(2,1)} %param.36) | copy-start | bytes 12292
  7.2 52.8 %copy-start.19 = (bf16[1024,256]{1,0:T(8,128)(2,1)S(1)}, bf16[1024,256]{1,0:T(8,128)(2,1)}, u32[]{:S(2)}) copy-start(bf16[1024,256]{1,0:T(8,128)(2,1)} %param.30) | copy-start | bytes 1572868
  7.2 49.9 %all-gather.5.cloned.1.call-start = ((), (), s32[]{:S(2)}) async-start(), calls=%async_computation.5 | async-start | bytes 2621440 | tf_op jit(solution)/shard_map/all_gather | solution.py:146
  7.9 182.9 %reduce-scatter.6.cloned.1.call-start = ((), (), s32[]{:S(2)}) async-start(), calls=%async_computation.6 | async-start | bytes 5242880 | tf_op jit(solution)/shard_map/reduce_scatter | solution.py:166
  28.4 38.9 %copy-start.21 = (bf16[1024,16]{0,1:T(8,128)(2,1)}, bf16[1024,16]{0,1:T(8,128)(2,1)S(1)}, u32[]{:S(2)}) copy-start(bf16[1024,16]{0,1:T(8,128)(2,1)S(1)} %all_gather.19) | copy-start | bytes 98308
  57.1 3.0 copy-start.40
  59.7 6.8 copy-start.17
  60.0 7.2 %copy-start.25 = (bf16[8,256]{1,0:T(8,128)(2,1)S(1)}, bf16[8,256]{1,0:T(8,128)(2,1)}, u32[]{:S(2)}) copy-start(bf16[8,256]{1,0:T(8,128)(2,1)} %param.35) | copy-start | bytes 12292
  60.9 10.5 %collective-permute-start = (bf16[512,512]{0,1:T(8,128)(2,1)S(1)}, bf16[512,512]{0,1:T(8,128)(2,1)S(1)}, u32[]{:S(2)}, u32[]{:S(2)}) collective-permute-start(bf16[512,512]{0,1:T(8,128)(2,1)S(1)} %get-tuple-element.203), channel_id=1, source_target_pairs={{0,4},{4,8},{8,12},{12,16},{16,20},{20,24},{24,28},{1,5},{5,9},{9,... | collective-permute-start | bytes 1572872 | tf_op jit(solution)/shard_map/ppermute | solution.py:26
  62.8 13.2 %collective-permute-start.1 = (bf16[512,512]{0,1:T(8,128)(2,1)S(1)}, bf16[512,512]{0,1:T(8,128)(2,1)S(1)}, u32[]{:S(2)}, u32[]{:S(2)}) collective-permute-start(bf16[512,512]{0,1:T(8,128)(2,1)S(1)} %get-tuple-element.204), channel_id=1, source_target_pairs={{4,0},{8,4},{12,8},{16,12},{20,16},{24,20},{28,24},{5,1},{9,5},{13... | collective-permute-start | bytes 1572872 | tf_op jit(solution)/shard_map/ppermute | solution.py:28
  110.6 4.1 copy-start.5
  114.6 0.7 copy-start.32
  114.6 0.7 copy-start.33
  114.6 79.4 %copy-start.34 = (bf16[1024]{0:T(1024)(128)(2,1)S(1)}, bf16[1024]{0:T(1024)(128)(2,1)}, u32[]{:S(2)}) copy-start(bf16[1024]{0:T(1024)(128)(2,1)} %param.42) | copy-start | bytes 6148
  114.7 125.8 %all-gather.7.cloned.1.call-start = ((), (), s32[]{:S(2)}) async-start(), calls=%async_computation.7 | async-start | bytes 2621440 | tf_op jit(solution)/shard_map/all_gather | solution.py:186
  193.8 142.3 %reduce-scatter.8.cloned.1.call-start = ((), (), s32[]{:S(2)}) async-start(), calls=%async_computation.8 | async-start | bytes 5242880 | tf_op jit(solution)/shard_map/reduce_scatter | solution.py:188
  240.4 15.6 %copy-start.39 = (bf16[1024,1024]{1,0:T(8,128)(2,1)S(1)}, bf16[1024,1024]{1,0:T(8,128)(2,1)}, u32[]{:S(2)}) copy-start(bf16[1024,1024]{1,0:T(8,128)(2,1)} %param.43) | copy-start | bytes 6291460
  252.8 2.0 copy-start.41
  252.8 3.3 copy-start.42
  260.4 0.7 copy-start.36
  260.4 0.7 copy-start.37
  260.4 128.7 %all-gather.9.cloned.1.call-start = ((), (), s32[]{:S(2)}) async-start(), calls=%async_computation.9 | async-start | bytes 2621440 | tf_op jit(solution)/shard_map/all_gather | solution.py:201
  336.1 3.2 copy-start.16
  340.5 1.0 copy-start.7
  342.5 133.7 %reduce-scatter.10.cloned.1.call-start = ((), (), s32[]{:S(2)}) async-start(), calls=%async_computation.10 | async-start | bytes 5242880 | tf_op jit(solution)/shard_map/reduce_scatter | solution.py:205
  400.5 75.7 %copy-start.8 = (f32[256,1024]{1,0:T(8,128)S(1)}, f32[256,1024]{1,0:T(8,128)}, u32[]{:S(2)}) copy-start(f32[256,1024]{1,0:T(8,128)} %copy-done.7) | copy-start | bytes 3145732
  400.5 126.7 %all-gather.11.cloned.1.call-start = ((), (), s32[]{:S(2)}) async-start(), calls=%async_computation.11 | async-start | bytes 2621440 | tf_op jit(solution)/shard_map/all_gather | solution.py:211
  479.5 53.5 %copy-start.9 = (f32[256,1024]{1,0:T(8,128)}, f32[256,1024]{1,0:T(8,128)S(1)}, u32[]{:S(2)}) copy-start(f32[256,1024]{1,0:T(8,128)S(1)} %get-tuple-element.185) | copy-start | bytes 3145732
  479.5 53.4 %copy-start.27 = (f32[256]{0:T(256)}, f32[256]{0:T(256)S(1)}, u32[]{:S(2)}) copy-start(f32[256]{0:T(256)S(1)} %negate_multiply_fusion.1) | copy-start | bytes 3076
  480.6 179.4 %reduce-scatter.14.cloned.1.call-start = ((), (), s32[]{:S(2)}) async-start(), calls=%async_computation.13 | async-start | bytes 40960 | tf_op jit(solution)/shard_map/reduce_scatter | solution.py:289
  480.8 52.1 %copy-start.6 = (bf16[1024,256]{0,1:T(8,128)(2,1)S(1)}, bf16[1024,256]{0,1:T(8,128)(2,1)}, u32[]{:S(2)}) copy-start(bf16[1024,256]{0,1:T(8,128)(2,1)} %copy-done.5) | copy-start | bytes 1572868
  538.3 6.3 copy-start.15
  544.8 11.5 %slice-start = ((s8[12582912]{0:T(1024)(128)(4,1)}), s8[4194304]{0:T(1024)(128)(4,1)S(1)}, s32[]{:S(2)}) async-start(s8[12582912]{0:T(1024)(128)(4,1)} %bitcast.128), calls=%async_computation.14 | async-start | bytes 8388608 | tf_op jit(solution)/shard_map/while
  544.8 11.5 %slice-start.1 = ((s8[12582912]{0:T(1024)(128)(4,1)}), s8[4194304]{0:T(1024)(128)(4,1)S(1)}, s32[]{:S(2)}) async-start(s8[12582912]{0:T(1024)(128)(4,1)} %bitcast.128), calls=%async_computation.15 | async-start | bytes 8388608 | tf_op jit(solution)/shard_map/while
  544.8 11.5 %slice-start.2 = ((s8[12582912]{0:T(1024)(128)(4,1)}), s8[4194304]{0:T(1024)(128)(4,1)S(1)}, s32[]{:S(2)}) async-start(s8[12582912]{0:T(1024)(128)(4,1)} %bitcast.128), calls=%async_computation.16 | async-start | bytes 8388608 | tf_op jit(solution)/shard_map/while
  563.2 2.2 copy-start.2
  566.1 2.0 copy-start.3
  566.1 2.2 copy-start.12
  568.4 0.8 copy-start.13
  574.5 6.3 copy-start.15
  581.0 11.5 %slice-start = ((s8[12582912]{0:T(1024)(128)(4,1)}), s8[4194304]{0:T(1024)(128)(4,1)S(1)}, s32[]{:S(2)}) async-start(s8[12582912]{0:T(1024)(128)(4,1)} %bitcast.128), calls=%async_computation.14 | async-start | bytes 8388608 | tf_op jit(solution)/shard_map/while
  581.0 11.5 %slice-start.1 = ((s8[12582912]{0:T(1024)(128)(4,1)}), s8[4194304]{0:T(1024)(128)(4,1)S(1)}, s32[]{:S(2)}) async-start(s8[12582912]{0:T(1024)(128)(4,1)} %bitcast.128), calls=%async_computation.15 | async-start | bytes 8388608 | tf_op jit(solution)/shard_map/while
  581.1 11.5 %slice-start.2 = ((s8[12582912]{0:T(1024)(128)(4,1)}), s8[4194304]{0:T(1024)(128)(4,1)S(1)}, s32[]{:S(2)}) async-start(s8[12582912]{0:T(1024)(128)(4,1)} %bitcast.128), calls=%async_computation.16 | async-start | bytes 8388608 | tf_op jit(solution)/shard_map/while
  599.4 2.2 copy-start.2
  602.3 2.0 copy-start.3
  602.3 2.2 copy-start.12
  604.6 0.8 copy-start.13
  605.4 8.5 %copy-start.14 = (bf16[2,512,256]{2,1,0:T(8,128)(2,1)S(1)}, bf16[2,512,256]{2,1,0:T(8,128)(2,1)}, u32[]{:S(2)}) copy-start(bf16[2,512,256]{2,1,0:T(8,128)(2,1)} %get-tuple-element.102) | copy-start | bytes 1572868
  605.4 8.5 %copy-start.26 = (bf16[8,256]{1,0:T(8,128)(2,1)S(1)}, bf16[8,256]{1,0:T(8,128)(2,1)}, u32[]{:S(2)}) copy-start(bf16[8,256]{1,0:T(8,128)(2,1)} %param.35) | copy-start | bytes 12292
  605.4 8.8 %copy-start.18 = (bf16[1024,256]{1,0:T(8,128)(2,1)S(1)}, bf16[1024,256]{1,0:T(8,128)(2,1)}, u32[]{:S(2)}) copy-start(bf16[1024,256]{1,0:T(8,128)(2,1)} %param.28) | copy-start | bytes 1572868
  608.1 10.5 %collective-permute-start.2 = (bf16[512,512]{0,1:T(8,128)(2,1)S(1)}, bf16[512,512]{0,1:T(8,128)(2,1)S(1)}, u32[]{:S(2)}, u32[]{:S(2)}) collective-permute-start(bf16[512,512]{0,1:T(8,128)(2,1)S(1)} %get-tuple-element.200), channel_id=1, source_target_pairs={{0,4},{4,8},{8,12},{12,16},{16,20},{20,24},{24,28},{1,5},{5,9},{9,... | collective-permute-start | bytes 1572872 | tf_op jit(solution)/shard_map/ppermute | solution.py:26
  610.0 13.2 %collective-permute-start.3 = (bf16[512,512]{0,1:T(8,128)(2,1)S(1)}, bf16[512,512]{0,1:T(8,128)(2,1)S(1)}, u32[]{:S(2)}, u32[]{:S(2)}) collective-permute-start(bf16[512,512]{0,1:T(8,128)(2,1)S(1)} %get-tuple-element.201), channel_id=1, source_target_pairs={{4,0},{8,4},{12,8},{16,12},{20,16},{24,20},{28,24},{5,1},{9,5},{13... | collective-permute-start | bytes 1572872 | tf_op jit(solution)/shard_map/ppermute | solution.py:28
  616.9 7.0 copy-start.4
  616.9 7.0 copy-start.38
  623.9 1.0 copy-start.20
  624.9 2.8 copy-start.11
  624.9 2.8 copy-start.30
  628.5 6.2 copy-start.22
  628.5 62.6 %copy-start.10 = (f32[256,1024]{1,0:T(8,128)S(1)}, f32[256,1024]{1,0:T(8,128)}, u32[]{:S(2)}) copy-start(f32[256,1024]{1,0:T(8,128)} %copy-done.9) | copy-start | bytes 3145732
  628.5 62.6 %copy-start.24 = (bf16[1024,16]{0,1:T(8,128)(2,1)S(1)}, bf16[1024,16]{0,1:T(8,128)(2,1)}, u32[]{:S(2)}) copy-start(bf16[1024,16]{0,1:T(8,128)(2,1)} %copy-done.23) | copy-start | bytes 98308
  628.6 62.6 %copy-start.28 = (f32[256]{0:T(256)S(1)}, f32[256]{0:T(256)}, u32[]{:S(2)}) copy-start(f32[256]{0:T(256)} %copy-done.27) | copy-start | bytes 3076
  628.6 62.6 %reduce-scatter.12.cloned.1.call-start = ((), (), s32[]{:S(2)}) async-start(), calls=%async_computation.12 | async-start | bytes 2621440 | tf_op jit(solution)/shard_map/reduce_scatter | solution.py:286
  628.6 64.7 %copy-start.1 = (bf16[1024,1024]{1,0:T(8,128)(2,1)S(1)}, bf16[1024,1024]{1,0:T(8,128)(2,1)}, u32[]{:S(2)}) copy-start(bf16[1024,1024]{1,0:T(8,128)(2,1)} %param.41) | copy-start | bytes 6291460
  (3 other events, 2.0 us)
Sparse Core Ops, SparseCore 0:
  9.6 47.4 all-gather.4
  114.8 76.0 reduce-scatter.5
  193.9 46.4 all-gather.6
  260.6 75.4 reduce-scatter.7
  342.6 46.4 all-gather.8
  400.6 75.4 reduce-scatter.9
  480.7 46.4 all-gather.10
  628.6 18.0 reduce-scatter.13
  649.1 42.0 reduce-scatter.11
where the time goes:
time: 711 us; the launch traced here: 700 us
  waiting for transfers between devices  441 us (62%)
  matrix products  118 us (17%)
  other arithmetic  43.8 us (6%)
  blocking collectives  36.4 us (5%)
  local copies, waits for them, and re-layouts  27.5 us (4%)
  between operations  14.8 us (2%)
  starting transfers between devices  12.1 us (2%)
    reduce_scatter x1, waiting for transfers between devices, shards(): lax.psum_scatter(times_transposed(grad_before, up_proj_weight), 'tensor',...  75.6 us
    reduce_scatter x1, waiting for transfers between devices, shards(): lax.psum_scatter(jnp.dot(attended, attention_out_weight, preferred_elemen...  75.6 us
    reduce_scatter x1, waiting for transfers between devices, shards(): lax.psum_scatter(jnp.dot(hidden, down_proj_weight, preferred_element_type...  75 us
    all_gather x1, waiting for transfers between devices, shards(): lax.all_gather(grad_ffn, 'tensor', axis=0, tiled=True)  46.6 us
    all_gather x1, waiting for transfers between devices, shards(): before = up_rows(lax.all_gather(middle_low, 'tensor', axis=0, tiled=True))  46.4 us
    all_gather x1, waiting for transfers between devices, shards(): lax.all_gather(grad_attn, 'tensor', axis=0, tiled=True)  46.3 us
    reduce_scatter x1, waiting for transfers between devices, shards(): lax.psum_scatter(tokens_term.astype(jnp.bfloat16), 'tensor', scatter_dime...  31.2 us
    all_gather x1, waiting for transfers between devices, shards(): lax.all_gather(tokens, 'tensor', axis=0, tiled=True)  28.7 us
  transfers between devices with their start and end apart: 13, of which 12 were waited for; matrix products, arithmetic and copies ran while one was open for 3% of the time, Pallas kernels for 0%

commit v1 on v0

v1 whole, which is shorter than its diff:
```python
import math

import jax
import jax.numpy as jnp
from jax import lax
from jax.experimental import pallas as pl
from jax.experimental.pallas import tpu as pltpu
from jax.sharding import PartitionSpec as P

MESH = pl.DeviceIdType.MESH
HD = 64
MAXLEN = 512
GROUP = 8
LANES = 128
NORM_EPS = 1e-05
MASKED = -1e30
LAG = 1
PLAN = (
    "+q0", "S0", "P20", "+q1", "Eq01", "Eq02", "S1", "Eq03", "T10", "S2", "Eq11", "+u0", "Eq12", "S3", "T11",
    "Eq13", "T12", "Eu01", "T13", "+u1", "P21", "Eu02", "P22", "T20", "Eu03", "P23", "T21", "Eu11", "Pn", "T22",
    "+o", "Eu12", "T23", "Eu13", "T30", "Eo1", "F", "P0", "T31", "+d0", "Eo2", "P4", "T32", "A0", "Eo3", "+d1",
    "A2", "T33", "A4", "Ed01", "A6", "Ed02", "Ed03", "L", "Pl", "Ed11", "B", "Ed12", "M", "U0", "U1", "Ed13", "U2",
    "U3", "D0", "D1", "D2", "D3",
)
F32 = jnp.float32
BF16 = jnp.bfloat16


def dot(left, right):
    return lax.dot_general(left, right, (((1,), (0,)), ((), ())), preferred_element_type=F32)


def dot_nt(left, right):
    return lax.dot_general(left, right, (((1,), (1,)), ((), ())), preferred_element_type=F32)


def tile(n):
    return pl.ds(pl.multiple_of(n * 256, 256), 256)


def layer_kernel(
    n_dp,
    x_in, cot_in, wq_in, wk_in, wv_in, wo_in, wup_in, wdn_in,
    len_in, qd_in, vd_in, qu_in, vu_in, qb_in, vb_in, ub_in, *rest
):
    vec_refs, rest = rest[:6], rest[6:]
    (
        out_ref, dx_ref, lora_ref,
        wqkv, wo, wup, wdn, small, lora_q, lora_v, vec_in, down_in,
        xwin, uwin, qwin, kwin, vwin, dowin, stwin, mask,
        att, attf, stat, midb, norm1, stat1, hid, gelp, acc, gffn, gbuf, dq, dk_acc, dv_acc, dkv,
        lsend, lrecv1, lrecv2,
        lsem, ssem, rsem,
    ) = rest
    rows = x_in.shape[0]
    width = x_in.shape[1]
    pairs = width // LANES
    dp, t = lax.axis_index("dp"), lax.axis_index("tensor")
    member = lax.rem(dp, GROUP)
    core = lax.rem(member, 2)
    yx = member // 2
    yx_x = yx + 1 - 2 * lax.rem(yx, 2)
    yx_y = yx + 2 - 4 * (yx // 2)
    yx_d = 3 - yx
    x_dev = (dp + 2 * (yx_x - yx), t)
    y_dev = (dp + 2 * (yx_y - yx), t)
    c_dev = (dp + 1 - 2 * core, t)

    def shard(a):
        first = jnp.where(t == 0, 1, t - 1)
        second = jnp.where(t == 0, 2, jnp.where(t == 3, 1, t + 1))
        third = jnp.where(t < 2, 3, 0)
        return jnp.where(a == 1, first, jnp.where(a == 2, second, third))

    barrier = pltpu.get_barrier_semaphore()
    for d in range(1, 4):
        pl.semaphore_signal(barrier, inc=1, device_id=(dp, lax.rem(t + d, 4)), device_id_type=MESH)
    for d in range(1, n_dp):
        pl.semaphore_signal(barrier, inc=1, device_id=(lax.rem(dp + d, n_dp), t), device_id_type=MESH)

    count = {"send": 0, "recv": 0, "local": 0}
    pending = []

    def alloc(kind, n):
        first = count[kind]
        count[kind] += n
        return first

    def when(pred, fn):
        if pred is None:
            fn()
        else:
            pl.when(pred)(fn)

    def remote(src, dst, recv, dev, pred=None):
        send = alloc("send", 1)
        copy = pltpu.make_async_remote_copy(
            src_ref=src, dst_ref=dst, send_sem=ssem.at[send], recv_sem=rsem.at[recv],
            device_id=dev, device_id_type=MESH,
        )
        when(pred, copy.start)
        pending.append((pred, copy))

    def arrived(dst, recv, pred=None):
        copy = pltpu.make_async_remote_copy(
            src_ref=dst, dst_ref=dst, send_sem=ssem.at[0], recv_sem=rsem.at[recv],
            device_id=(dp, t), device_id_type=MESH,
        )
        when(pred, copy.wait_recv)

    def local(src, dst):
        copy = pltpu.make_async_copy(src, dst, lsem.at[alloc("local", 1)])
        copy.start()
        return copy

    ld_qkv = [
        local(w, wqkv.at[t, :, :, :, pl.ds(256 * i, 256)]) for i, w in enumerate((wq_in, wk_in, wv_in))
    ]
    ld_x = [local(x_in, xwin.at[2])]
    ld_up = [local(wup_in, wup.at[t])]
    ld_o = [local(wo_in, wo.at[t])]
    ld_dn = [local(wdn_in, wdn.at[t])]
    ld_cot = [local(cot_in, gffn)]

    def done(copies):
        while copies:
            copies.pop().wait()

    class Chunk:
        def __init__(self, ref, first, size, loads):
            self.ref, self.first, self.size, self.loads = ref, first, size, loads
            self.zr = alloc("recv", 4)
            self.xr, self.yr, self.d1, self.d2, self.cr = (alloc("recv", 4) for _ in range(5))

        def region(self, s, place, lo=0, size=None):
            return self.ref.at[s, place, core, pl.ds(self.first + lo, size or self.size), :]

        def send(self):
            done(self.loads)
            own = self.region(t, yx)
            remote(own, own, self.zr + t, (dp, jnp.minimum(t + 1, 3)), t < 3)
            remote(own, own, self.zr + t, (dp, jnp.maximum(t - 1, 0)), t > 0)

        def stage0(self, a):
            s = shard(a)
            own = self.region(s, yx)
            arrived(own, self.zr + s)
            onward = jnp.where(s < t, t + 1, t - 1)
            remote(
                own, own, self.zr + s, (dp, jnp.clip(onward, 0, 3)),
                jnp.logical_and(onward >= 0, onward <= 3),
            )
            remote(own, own, self.xr + a, x_dev)
            remote(own, own, self.yr + a, y_dev)

        def stage1(self, a):
            s, half = shard(a), self.size // 2
            arrived(self.region(s, yx_x), self.xr + a)
            part = self.region(s, yx_x, 0, half)
            remote(part, part, self.d1 + a, y_dev)
            arrived(self.region(s, yx_y), self.yr + a)
            part = self.region(s, yx_y, half, half)
            remote(part, part, self.d2 + a, x_dev)

        def stage2(self, a):
            s, half = shard(a), self.size // 2
            arrived(self.region(s, yx_d, 0, half), self.d1 + a)
            arrived(self.region(s, yx_d, half, half), self.d2 + a)
            four = self.ref.at[s, :, core, pl.ds(self.first, self.size), :]
            remote(four, four, self.cr + a, c_dev)

        def stage3(self, a):
            s = shard(a)
            arrived(self.ref.at[s, :, 1 - core, pl.ds(self.first, self.size), :], self.cr + a)

    class Exchange:
        def __init__(self, ref, first, size):
            self.ref, self.first, self.size = ref, first, size
            self.base = alloc("recv", 6)

        def at(self, slot):
            return self.ref.at[slot, pl.ds(self.first, self.size), :]

        def go(self, src, dst, dev, pred):
            remote(self.at(src), self.at(dst), self.base + dst, dev, pred)

        def get(self, slot, pred):
            arrived(self.at(slot), self.base + slot, pred)

        def send(self, j):
            up, down = (dp, jnp.minimum(t + 1, 3)), (dp, jnp.maximum(t - 1, 0))
            if j == 1:
                self.go(2, 1, up, t < 3)
                self.go(2, 3, down, t > 0)
            if j == 2:
                self.go(1, 0, up, jnp.logical_and(t >= 1, t < 3))
                self.go(3, 4, down, jnp.logical_and(t > 0, t <= 2))
            if j == 3:
                self.go(0, 5, up, t == 2)
                self.go(4, 5, down, t == 1)

        def wait(self, j):
            if j == 1:
                self.get(1, t >= 1)
                self.get(3, t <= 2)
            if j == 2:
                self.get(0, t >= 2)
                self.get(4, t <= 1)
            if j == 3:
                self.get(5, jnp.logical_or(t == 0, t == 3))

        def send_far(self):
            after, before = (jnp.minimum(dp + 1, n_dp - 1), t), (jnp.maximum(dp - 1, 0), t)
            self.go(4, 0, after, jnp.logical_and(t <= 1, dp < n_dp - 1))
            self.go(0, 4, before, jnp.logical_and(t >= 2, dp > 0))

        def wait_far(self):
            self.get(0, jnp.logical_and(t <= 1, dp > 0))
            self.get(4, jnp.logical_and(t >= 2, dp < n_dp - 1))

        def send_near(self):
            after, before = (jnp.minimum(dp + 1, n_dp - 1), t), (jnp.maximum(dp - 1, 0), t)
            self.go(5, 1, after, jnp.logical_and(t == 0, dp < n_dp - 1))
            self.go(5, 3, before, jnp.logical_and(t == 3, dp > 0))

        def wait_near(self):
            self.get(1, jnp.logical_and(t == 0, dp > 0))
            self.get(3, jnp.logical_and(t == 3, dp < n_dp - 1))

    lane = lax.broadcasted_iota(jnp.int32, (1, LANES), 1)
    first_half = lane < HD

    def vec(i):
        return vec_in[i : i + 1, :]

    def halves(block):
        zero = jnp.zeros_like(block)
        return jnp.where(first_half, block, zero), jnp.where(first_half, zero, block)

    def clear(ref):
        @pl.when(jnp.logical_and(dp == 0, t <= 1))
        def _():
            ref[0] = jnp.zeros(ref.shape[1:], ref.dtype)

        @pl.when(jnp.logical_and(dp == 0, t == 0))
        def _():
            ref[1] = jnp.zeros(ref.shape[1:], ref.dtype)

        @pl.when(jnp.logical_and(dp == n_dp - 1, t >= 2))
        def _():
            ref[4] = jnp.zeros(ref.shape[1:], ref.dtype)

        @pl.when(jnp.logical_and(dp == n_dp - 1, t == 3))
        def _():
            ref[3] = jnp.zeros(ref.shape[1:], ref.dtype)

    def adapter(w):
        uwin[w] = dot_nt(xwin[w], down_in[...]).astype(BF16)

    def proj(w, pos, s):
        y = dot(xwin[w], wqkv[s].reshape(width, 3 * 256))
        u = uwin[w]
        place = (tile(pos), tile(s))
        q = y[:, :256] + dot(u, lora_q[s]) + small[s, 16:17, :]
        qwin[place] = (q * (1.0 / math.sqrt(HD))).astype(BF16)
        kwin[place] = y[:, 256:512].astype(BF16)
        v = y[:, 512:] + dot(u, lora_v[s]) + small[s, 17:18, :]
        vwin[place] = v.astype(BF16)

    def proj_all(w, pos):
        adapter(w)

        @pl.loop(0, 4, unroll=4)
        def _(s):
            proj(w, pos, s)

    def loop_pairs(lo, hi, body):
        @pl.loop(lo, hi, unroll=2)
        def _(p):
            body(p, pl.ds(pl.multiple_of(p * LANES, LANES), LANES))

    def column(index):
        return jnp.sum(jnp.where(lane == index, stat[...], 0.0), axis=1, keepdims=True)

    early = 4 * 256

    def attend(p, cols):
        q_heads = halves(qwin[tile(2), cols])
        k, v = kwin[0:early, cols], vwin[0:early, cols]
        outs, found = [], stat[...]
        for i in range(2):
            s = dot_nt(q_heads[i], k) + mask[:, 0:early]
            top = jnp.max(s, axis=1, keepdims=True)
            e = jnp.exp(s - top)
            total = jnp.sum(e, axis=1, keepdims=True)
            outs.append(dot(e.astype(BF16), v))
            found = jnp.where(lane == 2 * p + i, top, jnp.where(lane == 16 + 2 * p + i, total, found))
        attf[:, cols] = jnp.where(first_half, outs[0], outs[1])
        stat[...] = found

    def attend_last(p, cols):
        q_heads = halves(qwin[tile(2), cols])
        k, v = kwin[early:, cols], vwin[early:, cols]
        before, outs, found = attf[:, cols], [], stat[...]
        for i in range(2):
            old = column(2 * p + i)
            s = dot_nt(q_heads[i], k) + mask[:, early:]
            top = jnp.maximum(jnp.max(s, axis=1, keepdims=True), old)
            e = jnp.exp(s - top)
            alpha = jnp.exp(old - top)
            total = column(16 + 2 * p + i) * alpha + jnp.sum(e, axis=1, keepdims=True)
            outs.append((before * alpha + dot(e.astype(BF16), v)) * (1.0 / total))
            found = jnp.where(lane == 2 * p + i, top + jnp.log(total), found)
        o = jnp.where(first_half, outs[0], outs[1])
        attf[:, cols] = o
        att[:, cols] = o.astype(BF16)
        stat[...] = found

    def after_attention():
        @pl.loop(0, 4, unroll=4)
        def _(n):
            acc[:, tile(n)] = dot(att[...], wo[:, :, :, :, tile(n)].reshape(width, 256))

        z = xwin[2].astype(F32) + acc[...] + vec(0)
        centre = z - jnp.mean(z, axis=1, keepdims=True)
        r = lax.rsqrt(jnp.mean(centre * centre, axis=1, keepdims=True) + NORM_EPS)
        n1 = centre * r
        norm1[...] = n1
        stat1[...] = jnp.broadcast_to(r, stat1.shape)
        m = n1 * vec(1) + vec(2)
        midb[...] = m.astype(BF16)
        acc[...] = m + vec(3)

    def up(s):
        @pl.loop(0, 4, unroll=4)
        def _(n):
            b = dot(midb[...], wup[s, :, :, :, tile(n)].reshape(width, 256)) + small[s, pl.ds(18 + n, 1), :]
            cdf = 0.5 + 0.5 * lax.erf(b * (1.0 / math.sqrt(2.0)))
            hid[s, :, tile(n)] = (b * cdf).astype(BF16)
            gelp[s, :, tile(n)] = cdf + b * jnp.exp(-0.5 * b * b) * (1.0 / math.sqrt(2.0 * math.pi))

    def down(s):
        @pl.loop(0, 4, unroll=4)
        def _(n):
            acc[:, tile(n)] += dot(hid[s], wdn[s, :, :, :, tile(n)].reshape(width, 256))

    def second_norm():
        z = acc[...]
        centre = z - jnp.mean(z, axis=1, keepdims=True)
        r = lax.rsqrt(jnp.mean(centre * centre, axis=1, keepdims=True) + NORM_EPS)
        n2 = centre * r
        dk_acc[...] = n2 * vec(4) + vec(5)
        g = gffn[...].astype(F32) * vec(4)
        g = r * (g - jnp.mean(g, axis=1, keepdims=True) - n2 * jnp.mean(g * n2, axis=1, keepdims=True))
        acc[...] = g
        gffn[...] = g.astype(BF16)

    def ffn_back(s):
        @pl.loop(0, 4, unroll=4)
        def _(n):
            toward = dot_nt(gffn[...], wdn[s, n].reshape(256, width))
            gbuf[:, tile(n)] = (toward * gelp[s, :, tile(n)]).astype(BF16)

        @pl.loop(0, 4, unroll=4)
        def _(n):
            acc[:, tile(n)] += dot_nt(gbuf[...], wup[s, n].reshape(256, width))

    def first_norm_back():
        g = acc[...] * vec(1)
        n1 = norm1[...]
        g = g - jnp.mean(g, axis=1, keepdims=True) - n1 * jnp.mean(g * n1, axis=1, keepdims=True)
        g = stat1[:, 0:1] * g
        acc[...] = g
        gffn[...] = g.astype(BF16)

        @pl.loop(0, 4, unroll=4)
        def _(s):
            dowin[2, :, tile(s)] = dot_nt(gffn[...], wo[s].reshape(256, width)).astype(BF16)

        product = dowin[2].astype(F32) * attf[...]
        high = product.astype(BF16)
        low = (product - high.astype(F32)).astype(BF16)
        at_row = lax.broadcasted_iota(jnp.int32, (width, LANES), 0) // HD + 16
        at_lane = lax.broadcasted_iota(jnp.int32, (width, LANES), 1)
        pick = (at_row == at_lane).astype(F32).astype(BF16)
        delta = dot(high, pick) + dot(low, pick)
        both = jnp.where(lane < 16, stat[...], delta)
        stat[...] = both
        stwin[2] = both.T[0:32]

    def pass_queries(p, cols):
        q_heads, do_heads = halves(qwin[tile(2), cols]), halves(dowin[2, :, cols])
        k, v = kwin[:, cols], vwin[:, cols]
        parts = []
        for i in range(2):
            prob = jnp.exp(dot_nt(q_heads[i], k) + mask[...] - column(2 * p + i))
            ds = prob * (dot_nt(do_heads[i], v) - column(16 + 2 * p + i))
            parts.append(dot(ds.astype(BF16), k))
        dq[:, cols] = (jnp.where(first_half, parts[0], parts[1]) * (1.0 / math.sqrt(HD))).astype(BF16)

    def pass_keys(w, pos, lo, hi, first=False):
        def body(p, cols):
            k_heads, v_heads = halves(kwin[tile(2), cols]), halves(vwin[tile(2), cols])
            q, do = qwin[pos * 256 + lo : pos * 256 + hi, cols], dowin[w, lo:hi, cols]
            dk, dv = [], []
            for i in range(2):
                lse = stwin[w, pl.ds(2 * p + i, 1), :][:, lo:hi]
                delta = stwin[w, pl.ds(16 + 2 * p + i, 1), :][:, lo:hi]
                prob = jnp.exp(dot_nt(k_heads[i], q) + mask[:, pos * 256 + lo : pos * 256 + hi] - lse)
                ds = prob * (dot_nt(v_heads[i], do) - delta)
                dv.append(dot(prob.astype(BF16), do))
                dk.append(dot(ds.astype(BF16), q))
            dk, dv = jnp.where(first_half, dk[0], dk[1]), jnp.where(first_half, dv[0], dv[1])
            if first:
                dk_acc[:, cols] = dk
                dv_acc[:, cols] = dv
            else:
                dk_acc[:, cols] += dk
                dv_acc[:, cols] += dv

        loop_pairs(0, pairs, body)

    def lora_partial():
        u = uwin[2].astype(F32).T[0:16].astype(BF16)
        is_query = lax.broadcasted_iota(jnp.int32, (16, 1), 0) < 8
        for s in range(4):
            cols = slice(256 * s, 256 * s + 256)
            both = jnp.where(is_query, dot(u, dq[:, cols]), dot(u, dkv[1, :, cols]))
            lsend[s] = both

    def input_gradient():
        gu = jnp.zeros((rows, LANES), F32)
        for s in range(4):
            cols = slice(256 * s, 256 * s + 256)
            gu = gu + dot_nt(dq[:, cols], lora_q[s]) + dot_nt(dkv[1, :, cols], lora_v[s])
        gu = gu.astype(BF16)

        @pl.loop(0, 4, unroll=4)
        def _(n):
            total = acc[:, tile(n)] + dot(gu, down_in[:, tile(n)])
            for s in range(4):
                cols = slice(256 * s, 256 * s + 256)
                three = jnp.concatenate([dq[:, cols], dkv[0, :, cols], dkv[1, :, cols]], axis=1)
                total = total + dot_nt(three, wqkv[s, n].reshape(256, 3 * 256))
            norm1[:, tile(n)] = total

    def chunk(ref, first, size, loads):
        return Chunk(ref, first, size, loads)

    qkv0, qkv1 = chunk(wqkv, 0, 64, ld_qkv), chunk(wqkv, 64, 64, ld_qkv)
    up0, up1 = chunk(wup, 0, 64, ld_up), chunk(wup, 64, 64, ld_up)
    dn0, dn1 = chunk(wdn, 0, 64, ld_dn), chunk(wdn, 64, 64, ld_dn)
    o0 = chunk(wo, 0, 32, ld_o)
    half, quarter = rows // 2, rows // 4
    tok = [Exchange(xwin, i * quarter, quarter) for i in range(4)]
    small_base = alloc("recv", 4)
    wide = [Exchange(dowin, i * quarter, quarter) for i in range(4)]
    narrow = Exchange(stwin, 0, 32)
    lora1 = alloc("recv", 4)
    lora2 = alloc("recv", n_dp)

    clear(xwin)
    for i in range(8):
        cols = slice(LANES * i, LANES * i + LANES)
        for j, ref in enumerate(vec_refs):
            vec_in[j : j + 1, cols] = ref[i : i + 1, :].astype(F32)
    own_small = [2.0 * qu_in[...].astype(F32), 2.0 * vu_in[...].astype(F32)]
    small[t, 0:8, :] = own_small[0]
    small[t, 8:16, :] = own_small[1]
    for i in range(2):
        cols = slice(LANES * i, LANES * i + LANES)
        small[t, 16:17, cols] = qb_in[i : i + 1, :].astype(F32)
        small[t, 17:18, cols] = vb_in[i : i + 1, :].astype(F32)
        for j in range(4):
            small[t, 18 + j : 19 + j, cols] = ub_in[2 * j + i : 2 * j + i + 1, :].astype(F32)
    small[t, 22:24, :] = jnp.zeros((2, 256), F32)
    maps = [qd_in[...].astype(F32), vd_in[...].astype(F32), jnp.zeros((LANES - 16, width), F32)]
    down_in[...] = jnp.concatenate(maps, axis=0).astype(BF16)
    pl.semaphore_wait(barrier, 3 + n_dp - 1)
    done(ld_x)
    for d in range(1, 4):
        remote(small.at[t], small.at[t], small_base + t, (dp, lax.rem(t + d, 4)))

    near_first = jnp.where(t < 3, 3, 1)
    near_last = jnp.where(t < 3, 1, 3)
    blocks = {"0": (0, 0), "n": (near_first, 1), "2": (2, 2), "4": (4, 3), "l": (near_last, 4)}
    named = {"q0": qkv0, "q1": qkv1, "u0": up0, "u1": up1, "d0": dn0, "d1": dn1, "o": o0}
    events, waiting = [], []

    def run(entry):
        waiting.remove(entry)
        getattr(entry[1], "stage%d" % entry[3])(entry[2])

    def event(c, a):
        c.stage0(a)
        events.append((c, a))
        now = len(events)
        waiting.extend((now + k * LAG, c, a, k) for k in (1, 2, 3))
        for entry in sorted((e for e in waiting if e[0] <= now), key=lambda e: (e[0], e[3])):
            run(entry)

    def need(names, arrivals):
        cs = [named[n] for n in names]
        for entry in sorted((e for e in waiting if e[1] in cs and e[2] in arrivals), key=lambda e: (e[0], e[3])):
            run(entry)

    def setup():
        lengths = len_in[...]
        docs = lengths.shape[0] * LANES
        high, low = lengths // 256, lax.rem(lengths, 256)
        upto = (
            lax.broadcasted_iota(jnp.int32, (LANES, LANES), 0)
            <= lax.broadcasted_iota(jnp.int32, (LANES, LANES), 1)
        ).astype(F32).astype(BF16)

        def summed(part):
            return dot(part.astype(F32).astype(BF16), upto)

        ends = 256.0 * summed(high) + summed(low)
        window = mask.shape[1]
        first = (dp * 4 + t) * rows - MAXLEN
        spot = lax.broadcasted_iota(jnp.int32, (1, window), 1)
        nth = spot // rows
        nth = jnp.where(nth == 1, near_first, jnp.where(nth == 3, 4, jnp.where(nth == 4, near_last, nth)))
        position = first + nth * rows + lax.rem(spot, rows)
        place = position.astype(F32)
        passed = jnp.zeros((1, window), F32)
        before = jnp.zeros((1, 1), F32)
        for r in range(lengths.shape[0]):
            end = ends[r : r + 1, :] + before
            before = end[:, LANES - 1 :]
            column = jnp.broadcast_to(end, (LANES, LANES)).T[:, 0:1]
            passed = passed + jnp.sum((column <= place).astype(F32), axis=0, keepdims=True)
        inside = jnp.logical_and(position >= 0, passed < docs)
        ids = jnp.where(inside, passed, -1.0)
        own = jnp.broadcast_to(ids[:, 2 * rows : 3 * rows], (LANES, rows)).T[:, 0:1]
        mask[...] = jnp.where(own == ids, 0.0, MASKED)
        stat[...] = jnp.zeros(stat.shape, F32)

    def small_ready():
        for d in range(1, 4):
            peer = lax.rem(t + d, 4)
            arrived(small.at[peer], small_base + peer)
        none = jnp.zeros((8, 256), F32)
        lora_q[:, 16:, :] = jnp.zeros((4, LANES - 16, 256), BF16)
        lora_v[:, 16:, :] = jnp.zeros((4, LANES - 16, 256), BF16)
        for s in range(4):
            lora_q[s, 0:16, :] = jnp.concatenate([small[s, 0:8, :], none], axis=0).astype(BF16)
            lora_v[s, 0:16, :] = jnp.concatenate([none, small[s, 8:16, :]], axis=0).astype(BF16)

    everyone = (1, 2, 3)

    def part(a):
        return t if a == 0 else shard(a)

    for item in PLAN:
        kind, rest = item[0], item[1:]
        if kind == "+":
            named[rest].send()
        elif kind == "e":
            for a in everyone:
                event(named[rest], a)
        elif kind == "E":
            event(named[rest[:-1]], int(rest[-1]))
        elif kind == "S":
            tok[int(rest)].send(1)
        elif kind == "T":
            j, e = int(rest[0]), tok[int(rest[1])]
            e.wait(j)
            if j < 3:
                e.send(j + 1)
            if j == 2:
                e.send_far()
            if j == 3:
                e.send_near()
        elif kind == "F":
            for e in tok:
                e.wait_far()
        elif kind == "L":
            for e in tok:
                e.wait_near()
        elif kind == "N":
            need((rest[:-1],), (int(rest[-1]),) if rest[-1] != "*" else everyone)
        elif kind == "P":
            if rest[0] == "2":
                a = int(rest[1])
                if a == 0:
                    setup()
                    small_ready()
                    adapter(2)
                    done(ld_qkv)
                else:
                    need(("q0", "q1"), (a,))
                proj(2, 2, part(a))
            else:
                need(("q0", "q1"), everyone)
                proj_all(*blocks[rest[0]])
        elif kind == "A":
            loop_pairs(int(rest), int(rest) + 2, attend)
        elif kind == "B":
            loop_pairs(0, pairs, attend_last)
        elif kind == "M":
            need(("o",), everyone)
            done(ld_o)
            after_attention()
        elif kind == "U":
            a = int(rest)
            if a:
                need(("u0", "u1"), (a,))
            done(ld_up)
            up(part(a))
        elif kind == "D":
            a = int(rest)
            if a:
                need(("d0", "d1"), (a,))
            done(ld_dn)
            down(part(a))
    while waiting:
        run(min(waiting, key=lambda e: (e[0], e[3])))
    for copies in (ld_qkv, ld_o, ld_up, ld_dn):
        done(copies)

    done(ld_cot)
    second_norm()
    out_copy = local(dk_acc, out_ref)
    clear(dowin)
    clear(stwin)

    @pl.loop(0, 4, unroll=4)
    def _(s):
        ffn_back(s)

    first_norm_back()
    narrow.send(1)
    for e in wide:
        e.send(1)

    def turn(j, i):
        for e in [wide[i]] + ([narrow] if i == 0 else []):
            e.wait(j)
            if j < 3:
                e.send(j + 1)
            if j == 2:
                e.send_far()
            if j == 3:
                e.send_near()

    both = [narrow] + wide
    for i in range(4):
        loop_pairs(2 * i, 2 * i + 2, pass_queries)
        turn(1, i)
    out_copy.wait()
    pass_keys(2, 2, 0, rows, first=True)
    turn(2, 0)
    turn(2, 1)
    pass_keys(*blocks["n"], 0, rows)
    turn(2, 2)
    turn(2, 3)
    for e in both:
        e.wait_far()
    pass_keys(*blocks["0"], 0, rows)
    turn(3, 0)
    turn(3, 1)
    pass_keys(*blocks["4"], 0, rows)
    turn(3, 2)
    turn(3, 3)
    for e in both[:3]:
        e.wait_near()
    pass_keys(*blocks["l"], 0, half)
    for e in both[3:]:
        e.wait_near()
    pass_keys(*blocks["l"], half, rows)
    dkv[0] = dk_acc[...].astype(BF16)
    dkv[1] = dv_acc[...].astype(BF16)
    lora_partial()
    for d in range(1, 4):
        peer = lax.rem(t + d, 4)
        remote(lsend.at[peer], lrecv1.at[t], lora1 + t, (dp, peer))
    lrecv1[t] = lsend[t]
    input_gradient()
    dx_copy = local(norm1, dx_ref)
    for d in range(1, 4):
        peer = lax.rem(t + d, 4)
        arrived(lrecv1.at[peer], lora1 + peer)
    lrecv2[dp] = (lrecv1[0] + lrecv1[1]) + (lrecv1[2] + lrecv1[3])
    for d in range(1, n_dp):
        remote(lrecv2.at[dp], lrecv2.at[dp], lora2 + dp, (lax.rem(dp + d, n_dp), t))
    for d in range(1, n_dp):
        peer = lax.rem(dp + d, n_dp)
        arrived(lrecv2.at[peer], lora2 + peer)
    total = lrecv2[0]
    for i in range(1, n_dp):
        total = total + lrecv2[i]
    lora_ref[...] = total
    dx_copy.wait()
    for pred, copy in pending:
        when(pred, copy.wait_send)
    assert count["send"] <= ssem.shape[0] and count["recv"] <= rsem.shape[0]
    assert count["local"] <= lsem.shape[0]


def shards(
    tokens, document_lengths, query_proj_weight, query_proj_bias, key_proj_weight, value_proj_weight,
    value_proj_bias, query_adapter_down, value_adapter_down, query_adapter_up, value_adapter_up,
    attention_out_weight, attention_out_bias, attention_norm_gain, attention_norm_bias, up_proj_weight,
    up_proj_bias, down_proj_weight, down_proj_bias, feedforward_norm_gain, feedforward_norm_bias, cotangent,
):
    rows, width = tokens.shape
    n_dp = lax.axis_size("dp")
    window = rows + 2 * MAXLEN

    def fold(vector):
        return vector.reshape(vector.shape[0] // LANES, LANES)

    def cut(weight):
        return weight.reshape(4, 2, weight.shape[0] // GROUP, weight.shape[1])

    def vmem(shape, dtype):
        return pltpu.VMEM(shape, dtype)

    any_spec = pl.BlockSpec(memory_space=pl.ANY)
    vmem_spec = pl.BlockSpec(memory_space=pltpu.VMEM)
    full = (rows, width)
    rank = query_adapter_up.shape[0]
    call = pl.pallas_call(
        lambda *refs: layer_kernel(n_dp, *refs),
        out_shape=(
            jax.ShapeDtypeStruct(full, F32),
            jax.ShapeDtypeStruct(full, F32),
            jax.ShapeDtypeStruct((16, 256), F32),
        ),
        in_specs=[any_spec] * 8 + [vmem_spec] * 14,
        out_specs=(any_spec, any_spec, vmem_spec),
        scratch_shapes=[
            vmem((4, 4, 2, 128, 768), BF16),
            vmem((4, 4, 2, 32, 1024), BF16),
            vmem((4, 4, 2, 128, 1024), BF16),
            vmem((4, 4, 2, 128, 1024), BF16),
            vmem((4, 24, 256), F32),
            vmem((4, 128, 256), BF16),
            vmem((4, 128, 256), BF16),
            vmem((8, width), F32),
            vmem((LANES, width), BF16),
            vmem((6, rows, width), BF16),
            vmem((5, rows, LANES), BF16),
            vmem((window, width), BF16),
            vmem((window, width), BF16),
            vmem((window, width), BF16),
            vmem((6, rows, width), BF16),
            vmem((6, 32, rows), F32),
            vmem((rows, window), F32),
            vmem(full, BF16),
            vmem(full, F32),
            vmem((rows, LANES), F32),
            vmem(full, BF16),
            vmem(full, F32),
            vmem((rows, LANES), F32),
            vmem((4, rows, width), BF16),
            vmem((4, rows, width), F32),
            vmem(full, F32),
            vmem(full, BF16),
            vmem(full, BF16),
            vmem(full, BF16),
            vmem(full, F32),
            vmem(full, F32),
            vmem((2, rows, width), BF16),
            vmem((4, 16, 256), F32),
            vmem((4, 16, 256), F32),
            vmem((n_dp, 16, 256), F32),
            pltpu.SemaphoreType.DMA((16,)),
            pltpu.SemaphoreType.DMA((300 + n_dp,)),
            pltpu.SemaphoreType.DMA((260 + n_dp,)),
        ],
        compiler_params=pltpu.CompilerParams(
            collective_id=0, has_side_effects=True, vmem_limit_bytes=63 * 2**20
        ),
        name="layer",
    )
    out, grad, lora = call(
        tokens, cotangent, cut(query_proj_weight), cut(key_proj_weight), cut(value_proj_weight),
        cut(attention_out_weight), cut(up_proj_weight), cut(down_proj_weight), fold(document_lengths),
        query_adapter_down.T, value_adapter_down.T, query_adapter_up, value_adapter_up,
        fold(query_proj_bias), fold(value_proj_bias), fold(up_proj_bias), fold(attention_out_bias),
        fold(attention_norm_gain), fold(attention_norm_bias), fold(down_proj_bias), fold(feedforward_norm_gain),
        fold(feedforward_norm_bias),
    )
    lora = 2.0 * lora
    return out.astype(BF16), grad.astype(BF16), lora[:rank], lora[rank:]


def solution(mesh):
    whole, columns = P(), P(None, "tensor")
    stream = P(("dp", "tensor"), None)
    return jax.shard_map(
        shards,
        mesh=mesh,
        in_specs=(
            stream, whole, columns, P("tensor"), columns, columns, P("tensor"), whole, whole, columns, columns,
            P("tensor", None), whole, whole, whole, columns, P("tensor"), P("tensor", None), whole, whole, whole,
            stream,
        ),
        out_specs=(stream, stream, columns, columns),
        check_vma=False,
    )
```

time: 711 us -> 212 us (0.30)
  the two profiles are of different devices: /device:TPU:2 before, /device:TPU:0 now
where the time goes in v1:
time: 212 us; the launch traced here: 208 us
  Pallas kernels  203 us (96%)
  other arithmetic  3.77 us (2%)
    pallas_call x1, Pallas kernels, shards(): call(tokens, cotangent, cut(query_proj_weight), cut(key_proj_weight), cut...  203 us

profile of v1, /device:TPU:0, one launch (start us, length us, event | category | flops | bytes accessed | tf_op | source)
XLA Modules:
  0.0 208.2 jit_solution(8812086540031144926)
XLA Ops:
  0.6 202.9 %layer.1 = (f32[256,1024]{1,0:T(8,128)}, f32[256,1024]{1,0:T(8,128)}, f32[16,256]{1,0:T(8,128)}) custom-call(bf16[256,1024]{1,0:T(8,128)(2,1)} %refs_0_.1, bf16[256,1024]{1,0:T(8,128)(2,1)} %refs_1_.1, bf16[4,2,128,256]{3,2,1,0:T(8,128)(2,1)} %bitcast.20, bf16[4,2,128,256]{3,2,1,0:T(8,128)(2,1)} %bitcast.21, bf16[4,2,128,256]{3,2,1,0:T(8,128)(2,1)} %bitcast.22, ...), custom_call_target="tpu_custom_call" | custom-call | tf_op jit(solution)/shard_map/layer/pallas_call | solution.py:779
  203.6 0.0 copy-start
  203.6 2.2 %convert_element_type.6 = bf16[256,1024]{1,0:T(8,128)(2,1)} convert(f32[256,1024]{1,0:T(8,128)} %get-tuple-element.7) | non-fusion elementwise | flops 262144 | bytes 1572864 | tf_op jit(solution)/shard_map/convert_element_type | solution.py:788
  205.8 0.7 broadcast_multiply_fusion
  206.5 0.6 fusion
  207.1 0.0 copy-done
  207.1 0.9 convert_element_type.7
Async XLA Ops:
  203.6 3.5 %copy-start = (f32[256,1024]{1,0:T(8,128)S(1)}, f32[256,1024]{1,0:T(8,128)}, u32[]{:S(2)}) copy-start(f32[256,1024]{1,0:T(8,128)} %get-tuple-element.8) | copy-start | bytes 3145732
